TPU v7x, 256 devices: a whole 4x4x8 slice. The times are simulated.
256 devices in a mesh: fsdp: 64 (over z, y, core), rep: 4 (over x).
Axes of the slice: x: 4, y: 4, z: 8, core: 2. Of those that a mesh axis runs over, the one named last changes fastest.
Arguments:
- grads: float32 [64, 4, 192, 768], P(None, 'rep', 'fsdp'), may hold values from -9 to 9
- params: bfloat16 [64, 4, 192, 768], P(None, 'rep', 'fsdp'), may hold values from -3 to 3
- owner_slot: int32 [64], replicated, may hold values from 0 to 127, as said below
- left_stats: float32 [128, 768, 768], P('fsdp', 'rep'), may hold values from -0.1 to 1, as said below
- right_stats: float32 [128, 768, 768], P('fsdp', 'rep'), may hold values from -0.1 to 1, as said below
- left_root: float32 [128, 768, 768], P('fsdp', 'rep'), may hold values from -0.3 to 2, as said below
- right_root: float32 [128, 768, 768], P('fsdp', 'rep'), may hold values from -0.3 to 2, as said below
Outputs:
- new_params: bfloat16 [64, 4, 192, 768], P(None, 'rep', 'fsdp')
- update: float32 [64, 4, 192, 768], P(None, 'rep', 'fsdp')
- new_left_stats: float32 [128, 768, 768], P('fsdp', 'rep')
- new_right_stats: float32 [128, 768, 768], P('fsdp', 'rep')
Inputs may be any that keep to these rules, and one draw needn't show every extreme that they name: `owner_slot`: the 64 entries are distinct; slot s belongs to the device s // 2 of fsdp; in every draw some device of fsdp holds 2 blocks. `left_stats`: each slot's matrix is symmetric. `right_stats`: each slot's matrix is symmetric. `left_root`: each slot's matrix is symmetric. `right_root`: each slot's matrix is symmetric.
All inputs are finite; a program needn't handle non-finite values.
Results may differ from a plain program's by a relative error of at most 0.001.
Values sent between devices are 32-bit elements; how exact they have to be, the bound alone decides.
A program may use at most 64 MiB of HBM per device.

v0:
```python
import functools

import jax
import jax.numpy as jnp
from jax import lax
from jax.experimental import pallas as pl
from jax.experimental.pallas import tpu as pltpu
from jax.sharding import PartitionSpec as P

STAT_DECAY = 0.95
STEP_SIZE = 0.25
EPSILON = 1e-06
LANES = 128
VIA_MATE = ((2, 4, 6), (1, 3, 5, 7))
F32 = jnp.float32
BF16 = jnp.bfloat16
NN = (((1,), (0,)), ((), ()))
NT = (((1,), (1,)), ((), ()))


def split(value):
    high = value.astype(BF16)
    return high, (value - high.astype(F32)).astype(BF16)


def dot3(left, right, dims):
    dot = functools.partial(lax.dot_general, dimension_numbers=dims, preferred_element_type=F32)
    return dot(left[0], right[0]) + (dot(left[0], right[1]) + dot(left[1], right[0]))


def kernel(
    nf, nx, rows, groups, blocks,
    owner, grads, left_root, right_root, left_stats, right_stats,
    back, scales, new_left, new_right,
    owner_v, blocks_v, slot_block, grads_v, send, gath, ret, left_v, lstat_v, rstat_v,
    root_f, root_h, root_l, gh, gl, gt, lh, ll, mixed, lgh, lgl, sq, scale_v,
    in_sem, a_send, a_recv, r_send, r_recv, x_send, x_recv, f_send, f_recv,
    s_send, s_recv, u_send, u_recv, c_send, c_recv, turned,
):
    slots, stripe, width = left_v.shape
    panels = width // LANES
    half = width // 2
    packet = rows * panels
    size = nf // groups
    chunk = size * rows
    me = lax.axis_index("fsdp")
    x = lax.axis_index("rep")
    mz, mg = me // size, me % size
    right_x, left_x, far_x = (x + 1) % nx, (x + nx - 1) % nx, (x + 2) % nx
    h, pos = x // 2, x % 2
    mate = h * 2 + 1 - pos
    other = jnp.where(pos == 0, left_x, right_x)

    def at_x(target):
        return {"fsdp": me, "rep": target}

    def at_f(target):
        return {"fsdp": target, "rep": x}

    def remote(src, dst, send_sem, recv_sem, device):
        return pltpu.make_async_remote_copy(
            src_ref=src, dst_ref=dst, send_sem=send_sem, recv_sem=recv_sem,
            device_id=device, device_id_type=pl.DeviceIdType.MESH,
        )

    def await_bytes(ref, sem):
        pltpu.make_async_copy(ref, ref, sem).wait()

    order = [0]
    for step in range(groups // 2, 0, -1):
        order.append(step)
        if step != groups - step:
            order.append(groups - step)

    load_grads = pltpu.make_async_copy(grads, grads_v.at[pl.ds(0, blocks * packet)], in_sem.at[0])
    load_grads.start()
    load_owner = pltpu.make_async_copy(owner, owner_v, in_sem.at[9])
    load_owner.start()
    load_left = pltpu.make_async_copy(left_root, left_v, in_sem.at[1])
    load_left.start()
    loads_r = []
    for t in range(slots):
        for kind in range(2):
            col = h if kind == 0 else 1 - h
            cols = pl.ds(pl.multiple_of(col * half, LANES), half)
            src = right_root.at[t, :, cols]
            load = pltpu.make_async_copy(
                src, root_f.at[t, kind, pl.ds(pl.multiple_of(pos * stripe, 8), stripe)], in_sem.at[2 + 2 * t + kind]
            )
            load.start()
            loads_r.append(load)
    load_ls = pltpu.make_async_copy(left_stats, lstat_v, in_sem.at[6])
    load_ls.start()
    load_rs = pltpu.make_async_copy(right_stats, rstat_v, in_sem.at[7])
    load_rs.start()

    barrier = pltpu.get_barrier_semaphore()

    def greet(k, carry):
        pl.semaphore_signal(barrier, inc=1, device_id=at_f((me + k) % nf), device_id_type=pl.DeviceIdType.MESH)
        return carry

    lax.fori_loop(1, nf, greet, 0)
    for d in range(1, nx):
        pl.semaphore_signal(barrier, inc=1, device_id=at_x((x + d) % nx), device_id_type=pl.DeviceIdType.MESH)

    load_owner.wait()
    row = jnp.broadcast_to(owner_v[...], (blocks, blocks))
    down = lax.broadcasted_iota(jnp.int32, (blocks, blocks), 0)
    along = lax.broadcasted_iota(jnp.int32, (blocks, blocks), 1)
    column = jnp.sum(jnp.where(down == along, row, 0), axis=1, keepdims=True)
    slot_ids = lax.broadcasted_iota(jnp.int32, (blocks, slots * nf), 1)
    block_ids = lax.broadcasted_iota(jnp.int32, (blocks, slots * nf), 0)
    held = blocks + jnp.sum(jnp.where(column == slot_ids, block_ids - blocks, 0), axis=0, keepdims=True)
    blocks_v[...] = jnp.maximum(held, 0)
    to_smem = pltpu.make_async_copy(blocks_v, slot_block, in_sem.at[8])
    to_smem.start()
    pl.semaphore_wait(barrier, nf - 1 + nx - 1)

    def diag(t, kind, q):
        return root_f.at[t, kind, pl.ds(pl.multiple_of(q * stripe, 8), stripe), pl.ds(pl.multiple_of(q * LANES, LANES), 2 * LANES)]

    my_rows = pl.ds(pl.multiple_of(pos * stripe, 8), stripe)
    mate_rows = pl.ds(pl.multiple_of((1 - pos) * stripe, 8), stripe)

    def root_copy(t, kind):
        src, dst = (
            (diag(t, 0, pos), diag(t, 0, pos)),
            (root_f.at[t, 1, my_rows], root_f.at[t, 1, my_rows]),
            (root_f.at[t, 0, my_rows], root_f.at[t, 2, my_rows]),
            (diag(t, 0, 1 - pos), diag(t, 2, 1 - pos)),
        )[kind]
        return remote(src, dst, r_send.at[t, kind], r_recv.at[t, kind], at_x(mate if kind < 2 else other))

    def root_arrival(t, kind):
        ref = (
            diag(t, 0, 1 - pos), root_f.at[t, 1, mate_rows], root_f.at[t, 2, mate_rows], diag(t, 2, pos)
        )[kind]
        remote(ref, ref, r_send.at[t, kind], r_recv.at[t, kind], at_x(mate if kind < 2 else other)).wait_recv()

    for t in range(slots):
        loads_r[2 * t].wait()
        loads_r[2 * t + 1].wait()
        root_copy(t, 2).start()
        root_copy(t, 0).start()
        root_copy(t, 1).start()

    load_grads.wait()
    to_smem.wait()
    flat_grads = grads_v.reshape((blocks + 1) * packet, LANES)
    flat_grads[pl.ds(blocks * packet, packet), :] = jnp.zeros((packet, LANES), F32)
    flat_send = send.reshape(slots * nf * packet, LANES)

    def pack(t, dest):
        block = slot_block[0, slots * dest + t]
        for j in range(rows):
            value = flat_grads[pl.ds(block * packet + panels * j, panels), :]
            flat_send[pl.ds((t * nf + dest) * packet + j, panels, stride=rows), :] = value

    for t in range(slots):
        mine = gath.at[t, x, :, pl.ds(me * rows, rows)]
        pack(t, me)
        pltpu.make_async_copy(send.at[t, me], mine, a_recv.at[t, mz]).start()
        for offset in order:
            dz = (mz + offset) % groups

            def post(k, carry, t=t, dz=dz, mine=mine):
                dest = dz * size + (mg + k) % size
                pack(t, dest)
                remote(send.at[t, dest], mine, a_send.at[t], a_recv.at[t, mz], at_f(dest)).start()
                return carry

            lax.fori_loop(1 if offset == 0 else 0, size, post, 0)

    load_left.wait()
    for t in range(slots):
        for i in range(nx):
            lh[t, i], ll[t, i] = split(left_v[t, :, i * stripe : (i + 1) * stripe])

    def rows_of(k):
        source = (mz + groups - order[k]) % groups
        return source, pl.ds(source * chunk, chunk)

    sides = (mate, other)

    def direct(t, k, side):
        source, part = rows_of(k)
        ref = gath.at[t, x, :, part]
        return remote(ref, ref, x_send.at[t, side, k], x_recv.at[t, side, k], at_x(sides[side]))

    def arrival(t, k, side):
        source, part = rows_of(k)
        ref = gath.at[t, sides[side], :, part]
        return remote(ref, ref, x_send.at[t, side, k], x_recv.at[t, side, k], at_x(sides[side]))

    def forward(t, k):
        source, part = rows_of(k)
        to = 0 if k in VIA_MATE[t] else 1
        ref = gath.at[t, sides[1 - to], :, part]
        return remote(ref, ref, f_send.at[t, k], f_recv.at[t, k], at_x(sides[to]))

    def far_arrival(t, k):
        source, part = rows_of(k)
        ref = gath.at[t, far_x, :, part]
        return remote(ref, ref, f_send.at[t, k], f_recv.at[t, k], at_x(mate))

    def spread(t):
        for k in range(groups):
            source, part = rows_of(k)
            await_bytes(gath.at[t, x, :, part], a_recv.at[t, source])
            direct(t, k, 0).start()
            direct(t, k, 1).start()

    def relay(t):
        for k in range(groups):
            arrival(t, k, 1 if k in VIA_MATE[t] else 0).wait_recv()
            forward(t, k).start()

    def gather_rest(t):
        for k in range(groups):
            arrival(t, k, 0 if k in VIA_MATE[t] else 1).wait_recv()

    g4 = gath.reshape(slots, nx, panels, stripe, LANES)
    ret4 = ret.reshape(slots, panels, stripe, LANES)

    def take(t, i):
        total = jnp.zeros((1, LANES), F32)
        part = pl.ds(pl.multiple_of(i * stripe, 16), stripe)
        for c in range(panels):
            value = g4[t, i, c]
            total = total + jnp.sum(value * value, axis=0, keepdims=True)
            high, low = split(value)
            gh[t, part, c * LANES : (c + 1) * LANES] = high
            gl[t, part, c * LANES : (c + 1) * LANES] = low
        return total

    def mix(t, i, place):
        part = pl.ds(pl.multiple_of(i * stripe, 16), stripe)
        for c in range(2):
            cols = slice(c * half, (c + 1) * half)
            term = dot3((lh[t, i], ll[t, i]), (gh[t, part, cols], gl[t, part, cols]), NN)
            if place == 0:
                mixed[c] = term
            elif place < nx - 1:
                mixed[c] = mixed[c] + term
            else:
                lgh[c], lgl[c] = split(mixed[c] + term)

    per = half // LANES

    def precondition(t, near_part):
        near = (lgh[h], lgl[h])
        away = (lgh[1 - h], lgl[1 - h])
        root = [(root_h[t, kind], root_l[t, kind]) for kind in range(3)]
        if near_part:
            part = dot3(near, root[0], NN) + dot3(away, root[1], NT)
        else:
            part = dot3(near, root[1], NN) + dot3(away, root[2], NN)
        first = (h if near_part else 1 - h) * per
        for c in range(per):
            ret4[t, first + c] = part[:, c * LANES : (c + 1) * LANES]
        return jnp.sum(part * part, axis=0, keepdims=True)

    def square_send(t, squares):
        sq[t, x] = jnp.broadcast_to(jnp.sum(squares, axis=1, keepdims=True), sq.shape[2:])
        for d in range(1, nx):
            remote(sq.at[t, x], sq.at[t, x], s_send.at[t, d - 1], s_recv.at[t, d - 1], at_x((x + d) % nx)).start()

    def scale_of(t, grad_squares):
        for d in range(1, nx):
            ref = sq.at[t, (x + nx - d) % nx]
            remote(ref, ref, s_send.at[t, d - 1], s_recv.at[t, d - 1], at_x((x + d) % nx)).wait_recv()
        prec_mean = (((sq[t, 0] + sq[t, 1]) + sq[t, 2]) + sq[t, 3]) / (width * width)
        grad_mean = jnp.sum(grad_squares, axis=1, keepdims=True) / (width * width)
        scale_v[t] = jnp.sqrt(grad_mean / (prec_mean[0:1, :] + EPSILON))

    def to_all(post):
        for offset in order[1:] + order[:1]:
            dz = (mz + offset) % groups

            def body(k, carry, dz=dz):
                post(dz * size + (mg + k) % size)
                return carry

            lax.fori_loop(1 if offset == 0 else 0, size, body, 0)

    def give_back(t, part, first, count):
        span = pl.ds(first, count)

        def post(dest):
            src = ret.at[t, span, pl.ds(dest * rows, rows)]
            remote(src, back.at[t, me, span], u_send.at[part], u_recv.at[part], at_f(dest)).start()

        own = ret.at[t, span, pl.ds(me * rows, rows)]
        pltpu.make_async_copy(own, back.at[t, me, span], u_recv.at[part]).start()
        to_all(post)

    def give_scales():
        pltpu.make_async_copy(scale_v, scales.at[me], c_recv).start()
        to_all(lambda dest: remote(scale_v, scales.at[me], c_send, c_recv, at_f(dest)).start())

    def left_gram(t):
        mine = pl.ds(pl.multiple_of(x * stripe, 16), stripe)
        ours = (gh[t, mine], gl[t, mine])
        for n in range(3):
            part = slice(n * 256, (n + 1) * 256)
            gram = dot3(ours, (gh[t, part], gl[t, part]), NT)
            new_left[t, :, part] = STAT_DECAY * lstat_v[t, :, part] + (1.0 - STAT_DECAY) * gram

    def right_gram(t):
        first = (3 * x) // 2
        for i in range(nx):
            pair = jnp.concatenate([g4[t, i, first], g4[t, i, first + 1]], axis=1)
            gt[:, i * stripe : (i + 1) * stripe] = pair.T
        ours = split(gt[pl.ds(pl.multiple_of(pos * (LANES // 2), 8), stripe), :])
        for n in range(3):
            part = slice(n * 256, (n + 1) * 256)
            gram = dot3(ours, (gh[t, :, part], gl[t, :, part]), NN)
            new_right[t, :, part] = STAT_DECAY * rstat_v[t, :, part] + (1.0 - STAT_DECAY) * gram

    def mirror(t, kind, q):
        panel = pl.ds(pl.multiple_of((1 - q) * 2 * LANES, LANES), LANES)
        wide = root_f[t, kind, panel, pl.ds(pl.multiple_of(q * LANES, LANES), 2 * LANES)]
        turned[...] = wide.T
        part = turned[pl.ds(pl.multiple_of(q * (LANES // 2), 8), stripe), :]
        root_f[t, kind, pl.ds(pl.multiple_of(q * stripe, 8), stripe), panel] = part

    def take_root(t, kind):
        root_h[t, kind], root_l[t, kind] = split(root_f[t, kind])

    totals = [None] * slots
    root_arrival(0, 0)
    root_copy(0, 3).start()
    spread(0)
    root_arrival(0, 1)
    mirror(0, 0, 1 - pos)
    take_root(0, 0)
    take_root(0, 1)
    relay(0)
    spread(1)
    root_arrival(0, 2)
    root_arrival(0, 3)
    mirror(0, 2, pos)
    take_root(0, 2)
    totals[0] = take(0, x)
    mix(0, x, 0)
    gather_rest(0)
    for place, i in ((1, mate), (2, other)):
        totals[0] = totals[0] + take(0, i)
        mix(0, i, place)
    for k in range(groups):
        far_arrival(0, k).wait_recv()
    totals[0] = totals[0] + take(0, far_x)
    mix(0, far_x, 3)
    square_send(0, precondition(0, True) + precondition(0, False))
    give_back(0, 0, 0, panels)
    relay(1)
    root_arrival(1, 0)
    root_copy(1, 3).start()
    root_arrival(1, 1)
    mirror(1, 0, 1 - pos)
    take_root(1, 0)
    take_root(1, 1)
    scale_of(0, totals[0])
    load_ls.wait()
    left_gram(0)
    totals[1] = take(1, x)
    mix(1, x, 0)
    gather_rest(1)
    for place, i in ((1, mate), (2, other)):
        totals[1] = totals[1] + take(1, i)
        mix(1, i, place)
    for k in range(groups):
        far_arrival(1, k).wait_recv()
    totals[1] = totals[1] + take(1, far_x)
    mix(1, far_x, 3)
    squares = precondition(1, True)
    give_back(1, 1, h * per, per)
    root_arrival(1, 2)
    root_arrival(1, 3)
    mirror(1, 2, pos)
    take_root(1, 2)
    square_send(1, squares + precondition(1, False))
    give_back(1, 2, (1 - h) * per, per)
    scale_of(1, totals[1])
    give_scales()
    load_rs.wait()
    right_gram(0)
    left_gram(1)
    right_gram(1)
    await_bytes(back.at[0], u_recv.at[0])
    await_bytes(back.at[1, :, pl.ds(h * per, per)], u_recv.at[1])
    await_bytes(back.at[1, :, pl.ds((1 - h) * per, per)], u_recv.at[2])
    await_bytes(scales, c_recv)

    for t in range(slots):
        await_bytes(send.at[t, pl.ds(0, nf - 1)], a_send.at[t])
        for k in range(groups):
            direct(t, k, 0).wait_send()
            direct(t, k, 1).wait_send()
            forward(t, k).wait_send()
        for d in range(1, nx):
            remote(sq.at[t, x], sq.at[t, x], s_send.at[t, d - 1], s_recv.at[t, d - 1], at_x((x + d) % nx)).wait_send()
        for kind in range(4):
            root_copy(t, kind).wait_send()
    await_bytes(back.at[0, pl.ds(0, nf - 1)], u_send.at[0])
    await_bytes(back.at[1, pl.ds(0, nf - 1), pl.ds(0, per)], u_send.at[1])
    await_bytes(back.at[1, pl.ds(0, nf - 1), pl.ds(0, per)], u_send.at[2])
    await_bytes(scales.at[pl.ds(0, nf - 1)], c_send)


def finish(owner, back, scales, params, left, right, update, new_params, new_left, new_right, upd_t, sem):
    moves = (pltpu.make_async_copy(left, new_left, sem.at[0]), pltpu.make_async_copy(right, new_right, sem.at[1]))
    for move in moves:
        move.start()
    rows, blocks, width = params.shape
    panels = width // LANES
    packet = rows * panels
    slots = left.shape[0]
    nf = back.shape[0] // (packet * slots)

    def place(b, carry):
        slot = owner[b]
        start = ((slot % slots) * nf + slot // slots) * packet
        scale = scales[pl.ds(slot, 1), :]
        for c in range(panels):
            value = back[pl.ds(start + rows * c, rows), :] * scale
            update[pl.ds(b * packet + c, rows, stride=panels), :] = value
            upd_t[pl.ds(c * blocks + b, rows, stride=panels * blocks), :] = value
        return carry

    lax.fori_loop(0, blocks, place, 0, unroll=4)
    for j in range(rows):
        for c in range(panels):
            cols = slice(c * LANES, (c + 1) * LANES)
            step = STEP_SIZE * upd_t[(j * panels + c) * blocks : (j * panels + c + 1) * blocks, :]
            new_params[j, :, cols] = (params[j, :, cols].astype(F32) - step).astype(BF16)
    for move in moves:
        move.wait()


def on_device(grads, params, owner_slot, left_stats, right_stats, left_root, right_root):
    blocks, _, rows, width = grads.shape
    nf = lax.axis_size("fsdp")
    nx = lax.axis_size("rep")
    slots, stripe, _ = left_stats.shape
    panels = width // LANES
    half = width // 2
    packet = rows * panels
    groups = 8 if nf >= 64 else 2
    flat = grads.reshape(blocks * packet, 1, LANES)
    params_t = params.reshape(blocks, rows, width).transpose(1, 0, 2)
    hbm = pl.BlockSpec(memory_space=pltpu.HBM)
    vmem = pl.BlockSpec(memory_space=pltpu.VMEM)
    smem = pl.BlockSpec(memory_space=pltpu.SMEM)
    dma = pltpu.SemaphoreType.DMA
    back, scales, left, right = pl.pallas_call(
        functools.partial(kernel, nf, nx, rows, groups, blocks),
        out_shape=(
            pltpu.VMEM((slots, nf, panels, rows, 1, LANES), F32),
            pltpu.VMEM((nf, slots, 1, LANES), F32),
            pltpu.VMEM(left_stats.shape, F32),
            pltpu.VMEM(right_stats.shape, F32),
        ),
        in_specs=[hbm, hbm, hbm, hbm, hbm, hbm],
        out_specs=(vmem, vmem, vmem, vmem),
        scratch_shapes=[
            pltpu.VMEM((1, blocks), jnp.int32),
            pltpu.VMEM((1, slots * nf), jnp.int32),
            pltpu.SMEM((1, slots * nf), jnp.int32),
            pltpu.VMEM(((blocks + 1) * packet, 1, LANES), F32),
            pltpu.VMEM((slots, nf, panels, rows, 1, LANES), F32),
            pltpu.VMEM((slots, nx, panels, stripe, 1, LANES), F32),
            pltpu.VMEM((slots, panels, stripe, 1, LANES), F32),
            pltpu.VMEM((slots, stripe, width), F32),
            pltpu.VMEM((slots, stripe, width), F32),
            pltpu.VMEM((slots, stripe, width), F32),
            pltpu.VMEM((slots, 3, half, half), F32),
            pltpu.VMEM((slots, 3, half, half), BF16),
            pltpu.VMEM((slots, 3, half, half), BF16),
            pltpu.VMEM((slots, width, width), BF16),
            pltpu.VMEM((slots, width, width), BF16),
            pltpu.VMEM((2 * LANES, width), F32),
            pltpu.VMEM((slots, nx, stripe, stripe), BF16),
            pltpu.VMEM((slots, nx, stripe, stripe), BF16),
            pltpu.VMEM((2, stripe, half), F32),
            pltpu.VMEM((2, stripe, half), BF16),
            pltpu.VMEM((2, stripe, half), BF16),
            pltpu.VMEM((slots, nx, 8, LANES), F32),
            pltpu.VMEM((slots, 1, LANES), F32),
            dma((10,)),
            dma((slots,)),
            dma((slots, groups)),
            dma((slots, 4)),
            dma((slots, 4)),
            dma((slots, 2, groups)),
            dma((slots, 2, groups)),
            dma((slots, groups)),
            dma((slots, groups)),
            dma((slots, nx - 1)),
            dma((slots, nx - 1)),
            dma((3,)),
            dma((3,)),
            dma(()),
            dma(()),
            pltpu.VMEM((2 * LANES, LANES), F32),
        ],
        compiler_params=pltpu.CompilerParams(
            collective_id=0, has_side_effects=True, vmem_limit_bytes=60 * 1024 * 1024
        ),
    )(owner_slot.reshape(1, blocks), flat, left_root, right_root, left_stats, right_stats)
    update, new_params, new_left, new_right = pl.pallas_call(
        finish,
        out_shape=(
            jax.ShapeDtypeStruct((blocks * packet, LANES), F32),
            jax.ShapeDtypeStruct((rows, blocks, width), BF16),
            jax.ShapeDtypeStruct(left_stats.shape, F32),
            jax.ShapeDtypeStruct(right_stats.shape, F32),
        ),
        in_specs=[smem, vmem, vmem, vmem, vmem, vmem],
        out_specs=(vmem, vmem, hbm, hbm),
        scratch_shapes=[
            pltpu.VMEM((blocks * packet, LANES), F32),
            dma((2,)),
        ],
        compiler_params=pltpu.CompilerParams(vmem_limit_bytes=16 * 1024 * 1024),
    )(owner_slot, back.reshape(slots * nf * packet, LANES), scales.reshape(nf * slots, LANES), params_t, left, right)
    update = update.reshape(blocks, 1, rows, width)
    new_params = new_params.transpose(1, 0, 2).reshape(blocks, 1, rows, width)
    return (new_params, update, new_left, new_right)


def solution(mesh):
    in_specs = (
        P(None, "rep", "fsdp", None),
        P(None, "rep", "fsdp", None),
        P(),
        P("fsdp", "rep", None),
        P("fsdp", "rep", None),
        P("fsdp", "rep", None),
        P("fsdp", "rep", None),
    )
    out_specs = (
        P(None, "rep", "fsdp", None),
        P(None, "rep", "fsdp", None),
        P("fsdp", "rep", None),
        P("fsdp", "rep", None),
    )
    return jax.shard_map(
        on_device, mesh=mesh, in_specs=in_specs, out_specs=out_specs, check_vma=False
    )
```

profile of v0, /device:TPU:1, one launch (start us, length us, event | category | flops | bytes accessed | tf_op | source)
XLA Modules:
  0.0 94.8 jit_solution(5922130124757167091)
XLA Ops:
  0.6 0.0 copy-start
  0.6 0.0 copy-start.1
  0.7 91.3 %shard_map.102 = (f32[2,64,6,3,1,128]{5,4,3,2,1,0:T(1,128)S(1)}, f32[64,2,1,128]{3,2,1,0:T(1,128)S(1)}, f32[2,192,768]{2,1,0:T(8,128)S(1)}, f32[2,192,768]{2,1,0:T(8,128)S(1)}) custom-call(s32[1,64]{1,0:T(1,128)} %bitcast.14, f32[1152,1,128]{2,1,0:T(1,128)} %bitcast.15, f32[2,192,768]{2,1,0:T(8,128)} %left_root.1, f32[2,192,768]{2,1,0:T(8,128)} %right_root.1, ...), custom_call_target="tpu_custom_call" | custom-call | tf_op jit(solution)/shard_map/pallas_call | solution.py:457
  91.9 0.0 copy-done
  91.9 0.0 copy-done.1
  92.0 2.9 %shard_map.103 = (f32[1152,128]{1,0:T(8,128)}, bf16[3,64,768]{2,1,0:T(8,128)(2,1)}, f32[2,192,768]{2,1,0:T(8,128)}, f32[2,192,768]{2,1,0:T(8,128)}) custom-call(s32[64]{0:T(128)S(1)} %copy-done.1, f32[2304,128]{1,0:T(8,128)S(1)} %bitcast.11, f32[128,128]{1,0:T(8,128)S(1)} %bitcast.13, bf16[3,64,768]{2,1,0:T(8,128)(2,1)S(1)} %bitcast.12, ...), custom_call_target="tpu_custom_call" | custom-call | tf_op jit(solution)/shard_map/pallas_call | solution.py:512
Async XLA Ops:
  0.6 91.3 %copy-start = (bf16[64,1,3,768]{3,0,2,1:T(8,128)(2,1)S(1)}, bf16[64,1,3,768]{3,0,2,1:T(8,128)(2,1)}, u32[]{:S(2)}) copy-start(bf16[64,1,3,768]{3,0,2,1:T(8,128)(2,1)} %param.8) | copy-start | bytes 884740
  0.6 91.3 %copy-start.1 = (s32[64]{0:T(128)S(1)}, s32[64]{0:T(128)}, u32[]{:S(2)}) copy-start(s32[64]{0:T(128)} %owner.1) | copy-start | bytes 772
where the time goes:
time: 94.9 us; the launch traced here: 94.8 us
  Pallas kernels  94.1 us (99%)
    pallas_call x1, Pallas kernels, on_device(): pl.pallas_call(functools.partial(kernel, nf, nx, rows, groups, blocks), o...  91.3 us
    pallas_call x1, Pallas kernels, on_device(): pl.pallas_call(finish, out_shape=(jax.ShapeDtypeStruct((blocks * packet,...  2.87 us

commit v1 on v0

--- a/solution.py
+++ b/solution.py
@@ -32,15 +32,17 @@
     nf, nx, rows, groups, blocks,
     owner, grads, left_root, right_root, left_stats, right_stats,
     back, scales, new_left, new_right,
-    owner_v, blocks_v, slot_block, grads_v, send, gath, ret, left_v, lstat_v, rstat_v,
+    owner_v, blocks_v, slot_block, grads_v, send, last, send_last, gath, ret, left_v, lstat_v, rstat_v,
     root_f, root_h, root_l, gh, gl, gt, lh, ll, mixed, lgh, lgl, sq, scale_v,
     in_sem, a_send, a_recv, r_send, r_recv, x_send, x_recv, f_send, f_recv,
-    s_send, s_recv, u_send, u_recv, c_send, c_recv, turned,
+    s_send, s_recv, u_send, u_recv, c_send, c_recv, q_send, q_recv, p_send, p_recv, turned,
 ):
     slots, stripe, width = left_v.shape
     panels = width // LANES
     half = width // 2
     packet = rows * panels
+    front = panels - 1
+    sent = rows * front
     size = nf // groups
     chunk = size * rows
     me = lax.axis_index("fsdp")
@@ -115,6 +117,14 @@
     blocks_v[...] = jnp.maximum(held, 0)
     to_smem = pltpu.make_async_copy(blocks_v, slot_block, in_sem.at[8])
     to_smem.start()
+    load_grads.wait()
+    flat_grads = grads_v.reshape((blocks + 1) * packet, LANES)
+    flat_grads[pl.ds(blocks * packet, packet), :] = jnp.zeros((packet, LANES), F32)
+    flat_last = last.reshape(nx * (blocks + 1) * rows, LANES)
+    for i in range(nx):
+        flat_last[pl.ds((i * (blocks + 1) + blocks) * rows, rows), :] = jnp.zeros((rows, LANES), F32)
+    own_last = flat_grads[pl.ds(front, blocks * rows, stride=panels), :]
+    flat_last[pl.ds(x * (blocks + 1) * rows, blocks * rows), :] = own_last
     pl.semaphore_wait(barrier, nf - 1 + nx - 1)
 
     def diag(t, kind, q):
@@ -138,6 +148,19 @@
         )[kind]
         remote(ref, ref, r_send.at[t, kind], r_recv.at[t, kind], at_x(mate if kind < 2 else other)).wait_recv()
 
+    span = blocks * rows
+    low, high = pl.ds(0, span // 2), pl.ds(span // 2, span // 2)
+
+    def last_copy(kind):
+        ref = (last.at[x, pl.ds(0, span)], last.at[x, pl.ds(0, span)], last.at[other, low], last.at[mate, high])[kind]
+        return remote(ref, ref, q_send.at[kind], q_recv.at[kind], at_x(mate if kind % 2 == 0 else other))
+
+    def last_arrival(kind):
+        ref = (last.at[mate, pl.ds(0, span)], last.at[other, pl.ds(0, span)], last.at[far_x, low], last.at[far_x, high])[kind]
+        remote(ref, ref, q_send.at[kind], q_recv.at[kind], at_x(mate if kind % 2 == 0 else other)).wait_recv()
+
+    last_copy(0).start()
+    last_copy(1).start()
     for t in range(slots):
         loads_r[2 * t].wait()
         loads_r[2 * t + 1].wait()
@@ -145,26 +168,30 @@
         root_copy(t, 0).start()
         root_copy(t, 1).start()
 
-    load_grads.wait()
     to_smem.wait()
-    flat_grads = grads_v.reshape((blocks + 1) * packet, LANES)
-    flat_grads[pl.ds(blocks * packet, packet), :] = jnp.zeros((packet, LANES), F32)
-    flat_send = send.reshape(slots * nf * packet, LANES)
+    flat_send = send.reshape(slots * nf * sent, LANES)
+    flat_send_last = send_last.reshape(slots * nf * nx * rows, LANES)
 
     def pack(t, dest):
         block = slot_block[0, slots * dest + t]
         for j in range(rows):
-            value = flat_grads[pl.ds(block * packet + panels * j, panels), :]
-            flat_send[pl.ds((t * nf + dest) * packet + j, panels, stride=rows), :] = value
-
-    for t in range(slots):
-        mine = gath.at[t, x, :, pl.ds(me * rows, rows)]
+            value = flat_grads[pl.ds(block * packet + panels * j, front), :]
+            flat_send[pl.ds((t * nf + dest) * sent + j, front, stride=rows), :] = value
+
+    def pack_last(t, dest):
+        block = slot_block[0, slots * dest + t]
+        for i in range(nx):
+            value = flat_last[pl.ds((i * (blocks + 1) + block) * rows, rows), :]
+            flat_send_last[pl.ds(((t * nf + dest) * nx + i) * rows, rows), :] = value
+
+    def give_rows(t):
+        mine = gath.at[t, x, pl.ds(0, front), pl.ds(me * rows, rows)]
         pack(t, me)
         pltpu.make_async_copy(send.at[t, me], mine, a_recv.at[t, mz]).start()
         for offset in order:
             dz = (mz + offset) % groups
 
-            def post(k, carry, t=t, dz=dz, mine=mine):
+            def post(k, carry, dz=dz):
                 dest = dz * size + (mg + k) % size
                 pack(t, dest)
                 remote(send.at[t, dest], mine, a_send.at[t], a_recv.at[t, mz], at_f(dest)).start()
@@ -172,10 +199,27 @@
 
             lax.fori_loop(1 if offset == 0 else 0, size, post, 0)
 
-    load_left.wait()
-    for t in range(slots):
-        for i in range(nx):
-            lh[t, i], ll[t, i] = split(left_v[t, :, i * stripe : (i + 1) * stripe])
+    def give_last(t):
+        mine = gath.at[t, :, front, pl.ds(me * rows, rows)]
+        pack_last(t, me)
+        pltpu.make_async_copy(send_last.at[t, me], mine, p_recv.at[t]).start()
+        for offset in order:
+            dz = (mz + offset) % groups
+
+            def post(k, carry, dz=dz):
+                dest = dz * size + (mg + k) % size
+                pack_last(t, dest)
+                remote(send_last.at[t, dest], mine, p_send.at[t], p_recv.at[t], at_f(dest)).start()
+                return carry
+
+            lax.fori_loop(1 if offset == 0 else 0, size, post, 0)
+
+    def split_left():
+        load_left.wait()
+        for t in range(slots):
+            for i in range(nx):
+                lh[t, i], ll[t, i] = split(left_v[t, :, i * stripe : (i + 1) * stripe])
+
 
     def rows_of(k):
         source = (mz + groups - order[k]) % groups
@@ -185,29 +229,29 @@
 
     def direct(t, k, side):
         source, part = rows_of(k)
-        ref = gath.at[t, x, :, part]
+        ref = gath.at[t, x, pl.ds(0, front), part]
         return remote(ref, ref, x_send.at[t, side, k], x_recv.at[t, side, k], at_x(sides[side]))
 
     def arrival(t, k, side):
         source, part = rows_of(k)
-        ref = gath.at[t, sides[side], :, part]
+        ref = gath.at[t, sides[side], pl.ds(0, front), part]
         return remote(ref, ref, x_send.at[t, side, k], x_recv.at[t, side, k], at_x(sides[side]))
 
     def forward(t, k):
         source, part = rows_of(k)
         to = 0 if k in VIA_MATE[t] else 1
-        ref = gath.at[t, sides[1 - to], :, part]
+        ref = gath.at[t, sides[1 - to], pl.ds(0, front), part]
         return remote(ref, ref, f_send.at[t, k], f_recv.at[t, k], at_x(sides[to]))
 
     def far_arrival(t, k):
         source, part = rows_of(k)
-        ref = gath.at[t, far_x, :, part]
+        ref = gath.at[t, far_x, pl.ds(0, front), part]
         return remote(ref, ref, f_send.at[t, k], f_recv.at[t, k], at_x(mate))
 
     def spread(t):
         for k in range(groups):
             source, part = rows_of(k)
-            await_bytes(gath.at[t, x, :, part], a_recv.at[t, source])
+            await_bytes(gath.at[t, x, pl.ds(0, front), part], a_recv.at[t, source])
             direct(t, k, 0).start()
             direct(t, k, 1).start()
 
@@ -329,19 +373,31 @@
         root_h[t, kind], root_l[t, kind] = split(root_f[t, kind])
 
     totals = [None] * slots
+    give_rows(0)
+    for kind in range(2):
+        last_arrival(kind)
+    for kind in range(2, 4):
+        last_copy(kind).start()
     root_arrival(0, 0)
     root_copy(0, 3).start()
+    give_rows(1)
+    split_left()
     spread(0)
+    for kind in range(2, 4):
+        last_arrival(kind)
+    give_last(0)
     root_arrival(0, 1)
     mirror(0, 0, 1 - pos)
     take_root(0, 0)
     take_root(0, 1)
     relay(0)
     spread(1)
+    give_last(1)
     root_arrival(0, 2)
     root_arrival(0, 3)
     mirror(0, 2, pos)
     take_root(0, 2)
+    await_bytes(gath.at[0, :, front], p_recv.at[0])
     totals[0] = take(0, x)
     mix(0, x, 0)
     gather_rest(0)
@@ -364,6 +420,7 @@
     scale_of(0, totals[0])
     load_ls.wait()
     left_gram(0)
+    await_bytes(gath.at[1, :, front], p_recv.at[1])
     totals[1] = take(1, x)
     mix(1, x, 0)
     gather_rest(1)
@@ -407,6 +464,10 @@
     await_bytes(back.at[1, pl.ds(0, nf - 1), pl.ds(0, per)], u_send.at[1])
     await_bytes(back.at[1, pl.ds(0, nf - 1), pl.ds(0, per)], u_send.at[2])
     await_bytes(scales.at[pl.ds(0, nf - 1)], c_send)
+    for kind in range(4):
+        last_copy(kind).wait_send()
+    for t in range(slots):
+        await_bytes(send_last.at[t, pl.ds(0, nf - 1)], p_send.at[t])
 
 
 def finish(owner, back, scales, params, left, right, update, new_params, new_left, new_right, upd_t, sem):
@@ -469,7 +530,9 @@
             pltpu.VMEM((1, slots * nf), jnp.int32),
             pltpu.SMEM((1, slots * nf), jnp.int32),
             pltpu.VMEM(((blocks + 1) * packet, 1, LANES), F32),
-            pltpu.VMEM((slots, nf, panels, rows, 1, LANES), F32),
+            pltpu.VMEM((slots, nf, panels - 1, rows, 1, LANES), F32),
+            pltpu.VMEM((nx, (blocks + 1) * rows, 1, LANES), F32),
+            pltpu.VMEM((slots, nf, nx, rows, 1, LANES), F32),
             pltpu.VMEM((slots, nx, panels, stripe, 1, LANES), F32),
             pltpu.VMEM((slots, panels, stripe, 1, LANES), F32),
             pltpu.VMEM((slots, stripe, width), F32),
@@ -503,6 +566,10 @@
             dma((3,)),
             dma(()),
             dma(()),
+            dma((4,)),
+            dma((4,)),
+            dma((slots,)),
+            dma((slots,)),
             pltpu.VMEM((2 * LANES, LANES), F32),
         ],
         compiler_params=pltpu.CompilerParams(

time: 94.9 us -> 92.5 us (0.975)
  Pallas kernels: 94.1 us -> 91.7 us
    pallas_call x1, Pallas kernels: 91.3 us -> 88.8 us  [on_device(): pl.pallas_call(functools.partial(kernel, nf, nx, rows, groups, blocks), o...]
where the time goes in v1:
time: 92.5 us; the launch traced here: 92.4 us
  Pallas kernels  91.7 us (99%)
    pallas_call x1, Pallas kernels, on_device(): pl.pallas_call(functools.partial(kernel, nf, nx, rows, groups, blocks), o...  88.8 us
    pallas_call x1, Pallas kernels, on_device(): pl.pallas_call(finish, out_shape=(jax.ShapeDtypeStruct((blocks * packet,...  2.87 us

profile of v1, /device:TPU:1, one launch (start us, length us, event | category | flops | bytes accessed | tf_op | source)
XLA Modules:
  0.0 92.4 jit_solution(420290454715725835)
XLA Ops:
  0.6 0.0 copy-start
  0.6 0.0 copy-start.1
  0.7 88.8 %shard_map.102 = (f32[2,64,6,3,1,128]{5,4,3,2,1,0:T(1,128)S(1)}, f32[64,2,1,128]{3,2,1,0:T(1,128)S(1)}, f32[2,192,768]{2,1,0:T(8,128)S(1)}, f32[2,192,768]{2,1,0:T(8,128)S(1)}) custom-call(s32[1,64]{1,0:T(1,128)} %bitcast.14, f32[1152,1,128]{2,1,0:T(1,128)} %bitcast.15, f32[2,192,768]{2,1,0:T(8,128)} %left_root.1, f32[2,192,768]{2,1,0:T(8,128)} %right_root.1, ...), custom_call_target="tpu_custom_call" | custom-call | tf_op jit(solution)/shard_map/pallas_call | solution.py:518
  89.5 0.0 copy-done
  89.5 0.0 copy-done.1
  89.5 2.9 %shard_map.103 = (f32[1152,128]{1,0:T(8,128)}, bf16[3,64,768]{2,1,0:T(8,128)(2,1)}, f32[2,192,768]{2,1,0:T(8,128)}, f32[2,192,768]{2,1,0:T(8,128)}) custom-call(s32[64]{0:T(128)S(1)} %copy-done.1, f32[2304,128]{1,0:T(8,128)S(1)} %bitcast.11, f32[128,128]{1,0:T(8,128)S(1)} %bitcast.13, bf16[3,64,768]{2,1,0:T(8,128)(2,1)S(1)} %bitcast.12, ...), custom_call_target="tpu_custom_call" | custom-call | tf_op jit(solution)/shard_map/pallas_call | solution.py:579
Async XLA Ops:
  0.6 88.9 %copy-start = (bf16[64,1,3,768]{3,0,2,1:T(8,128)(2,1)S(1)}, bf16[64,1,3,768]{3,0,2,1:T(8,128)(2,1)}, u32[]{:S(2)}) copy-start(bf16[64,1,3,768]{3,0,2,1:T(8,128)(2,1)} %param.8) | copy-start | bytes 884740
  0.6 88.9 %copy-start.1 = (s32[64]{0:T(128)S(1)}, s32[64]{0:T(128)}, u32[]{:S(2)}) copy-start(s32[64]{0:T(128)} %owner.1) | copy-start | bytes 772

commit v2 on v1

--- a/solution.py
+++ b/solution.py
@@ -166,7 +166,8 @@
         loads_r[2 * t + 1].wait()
         root_copy(t, 2).start()
         root_copy(t, 0).start()
-        root_copy(t, 1).start()
+        if t == 0:
+            root_copy(t, 1).start()
 
     to_smem.wait()
     flat_send = send.reshape(slots * nf * sent, LANES)
@@ -392,6 +393,7 @@
     take_root(0, 1)
     relay(0)
     spread(1)
+    root_copy(1, 1).start()
     give_last(1)
     root_arrival(0, 2)
     root_arrival(0, 3)
@@ -470,7 +472,7 @@
         await_bytes(send_last.at[t, pl.ds(0, nf - 1)], p_send.at[t])
 
 
-def finish(owner, back, scales, params, left, right, update, new_params, new_left, new_right, upd_t, sem):
+def finish(owner, back, scales, params, left, right, update, new_params, new_left, new_right, upd_t, upd_v, par_v, sem):
     moves = (pltpu.make_async_copy(left, new_left, sem.at[0]), pltpu.make_async_copy(right, new_right, sem.at[1]))
     for move in moves:
         move.start()
@@ -486,16 +488,29 @@
         scale = scales[pl.ds(slot, 1), :]
         for c in range(panels):
             value = back[pl.ds(start + rows * c, rows), :] * scale
-            update[pl.ds(b * packet + c, rows, stride=panels), :] = value
+            upd_v[pl.ds(b * packet + c, rows, stride=panels), :] = value
             upd_t[pl.ds(c * blocks + b, rows, stride=panels * blocks), :] = value
         return carry
 
-    lax.fori_loop(0, blocks, place, 0, unroll=4)
-    for j in range(rows):
-        for c in range(panels):
-            cols = slice(c * LANES, (c + 1) * LANES)
-            step = STEP_SIZE * upd_t[(j * panels + c) * blocks : (j * panels + c + 1) * blocks, :]
-            new_params[j, :, cols] = (params[j, :, cols].astype(F32) - step).astype(BF16)
+    quarter = blocks // 4
+    outs = []
+    for q in range(4):
+        lax.fori_loop(q * quarter, (q + 1) * quarter, place, 0, unroll=4)
+        some = pl.ds(q * quarter * packet, quarter * packet)
+        outs.append(pltpu.make_async_copy(upd_v.at[some], update.at[some], sem.at[2 + q]))
+        outs[-1].start()
+        part = slice(q * quarter, (q + 1) * quarter)
+        for j in range(rows):
+            for c in range(panels):
+                cols = slice(c * LANES, (c + 1) * LANES)
+                first = (j * panels + c) * blocks + q * quarter
+                step = STEP_SIZE * upd_t[first : first + quarter, :]
+                par_v[j, part, cols] = (params[j, part, cols].astype(F32) - step).astype(BF16)
+        some = pl.ds(q * quarter, quarter)
+        outs.append(pltpu.make_async_copy(par_v.at[:, some], new_params.at[:, some], sem.at[6 + q]))
+        outs[-1].start()
+    for out in outs:
+        out.wait()
     for move in moves:
         move.wait()
 
@@ -585,10 +600,12 @@
             jax.ShapeDtypeStruct(right_stats.shape, F32),
         ),
         in_specs=[smem, vmem, vmem, vmem, vmem, vmem],
-        out_specs=(vmem, vmem, hbm, hbm),
+        out_specs=(hbm, hbm, hbm, hbm),
         scratch_shapes=[
             pltpu.VMEM((blocks * packet, LANES), F32),
-            dma((2,)),
+            pltpu.VMEM((blocks * packet, LANES), F32),
+            pltpu.VMEM((rows, blocks, width), BF16),
+            dma((10,)),
         ],
         compiler_params=pltpu.CompilerParams(vmem_limit_bytes=16 * 1024 * 1024),
     )(owner_slot, back.reshape(slots * nf * packet, LANES), scales.reshape(nf * slots, LANES), params_t, left, right)

time: 92.5 us -> 91.3 us (0.987)
  Pallas kernels: 91.7 us -> 90.5 us
where the time goes in v2:
time: 91.3 us; the launch traced here: 91.2 us
  Pallas kernels  90.5 us (99%)
    pallas_call x1, Pallas kernels, on_device(): pl.pallas_call(functools.partial(kernel, nf, nx, rows, groups, blocks), o...  88.2 us
    pallas_call x1, Pallas kernels, on_device(): pl.pallas_call(finish, out_shape=(jax.ShapeDtypeStruct((blocks * packet,...  2.33 us

profile of v2, /device:TPU:1, one launch (start us, length us, event | category | flops | bytes accessed | tf_op | source)
XLA Modules:
  0.0 91.2 jit_solution(3281717983315845905)
XLA Ops:
  0.6 0.0 copy-start
  0.6 0.0 copy-start.1
  0.7 88.2 %shard_map.102 = (f32[2,64,6,3,1,128]{5,4,3,2,1,0:T(1,128)S(1)}, f32[64,2,1,128]{3,2,1,0:T(1,128)S(1)}, f32[2,192,768]{2,1,0:T(8,128)S(1)}, f32[2,192,768]{2,1,0:T(8,128)S(1)}) custom-call(s32[1,64]{1,0:T(1,128)} %bitcast.14, f32[1152,1,128]{2,1,0:T(1,128)} %bitcast.15, f32[2,192,768]{2,1,0:T(8,128)} %left_root.1, f32[2,192,768]{2,1,0:T(8,128)} %right_root.1, ...), custom_call_target="tpu_custom_call" | custom-call | tf_op jit(solution)/shard_map/pallas_call | solution.py:533
  88.8 0.0 copy-done
  88.9 0.0 copy-done.1
  88.9 2.3 %shard_map.103 = (f32[1152,128]{1,0:T(8,128)}, bf16[3,64,768]{2,1,0:T(8,128)(2,1)}, f32[2,192,768]{2,1,0:T(8,128)}, f32[2,192,768]{2,1,0:T(8,128)}) custom-call(s32[64]{0:T(128)S(1)} %copy-done.1, f32[2304,128]{1,0:T(8,128)S(1)} %bitcast.11, f32[128,128]{1,0:T(8,128)S(1)} %bitcast.13, bf16[3,64,768]{2,1,0:T(8,128)(2,1)S(1)} %bitcast.12, ...), custom_call_target="tpu_custom_call" | custom-call | tf_op jit(solution)/shard_map/pallas_call | solution.py:594
Async XLA Ops:
  0.6 88.2 %copy-start = (bf16[64,1,3,768]{3,0,2,1:T(8,128)(2,1)S(1)}, bf16[64,1,3,768]{3,0,2,1:T(8,128)(2,1)}, u32[]{:S(2)}) copy-start(bf16[64,1,3,768]{3,0,2,1:T(8,128)(2,1)} %param.8) | copy-start | bytes 884740
  0.6 88.2 %copy-start.1 = (s32[64]{0:T(128)S(1)}, s32[64]{0:T(128)}, u32[]{:S(2)}) copy-start(s32[64]{0:T(128)} %owner.1) | copy-start | bytes 772

commit v3 on v2

--- a/solution.py
+++ b/solution.py
@@ -78,8 +78,6 @@
     load_grads.start()
     load_owner = pltpu.make_async_copy(owner, owner_v, in_sem.at[9])
     load_owner.start()
-    load_left = pltpu.make_async_copy(left_root, left_v, in_sem.at[1])
-    load_left.start()
     loads_r = []
     for t in range(slots):
         for kind in range(2):
@@ -91,10 +89,6 @@
             )
             load.start()
             loads_r.append(load)
-    load_ls = pltpu.make_async_copy(left_stats, lstat_v, in_sem.at[6])
-    load_ls.start()
-    load_rs = pltpu.make_async_copy(right_stats, rstat_v, in_sem.at[7])
-    load_rs.start()
 
     barrier = pltpu.get_barrier_semaphore()
 
@@ -168,6 +162,13 @@
         root_copy(t, 0).start()
         if t == 0:
             root_copy(t, 1).start()
+
+    load_left = pltpu.make_async_copy(left_root, left_v, in_sem.at[1])
+    load_left.start()
+    load_ls = pltpu.make_async_copy(left_stats, lstat_v, in_sem.at[6])
+    load_ls.start()
+    load_rs = pltpu.make_async_copy(right_stats, rstat_v, in_sem.at[7])
+    load_rs.start()
 
     to_smem.wait()
     flat_send = send.reshape(slots * nf * sent, LANES)

time: 91.3 us -> 91.3 us (level)
  no operation moved by 1% of the time
where the time goes in v3:
time: 91.3 us; the launch traced here: 91.2 us
  Pallas kernels  90.5 us (99%)
    pallas_call x1, Pallas kernels, on_device(): pl.pallas_call(functools.partial(kernel, nf, nx, rows, groups, blocks), o...  88.2 us
    pallas_call x1, Pallas kernels, on_device(): pl.pallas_call(finish, out_shape=(jax.ShapeDtypeStruct((blocks * packet,...  2.33 us

profile of v3, /device:TPU:1, one launch (start us, length us, event | category | flops | bytes accessed | tf_op | source)
XLA Modules:
  0.0 91.2 jit_solution(6633967338074939738)
XLA Ops:
  0.6 0.0 copy-start
  0.6 0.0 copy-start.1
  0.7 88.2 %shard_map.102 = (f32[2,64,6,3,1,128]{5,4,3,2,1,0:T(1,128)S(1)}, f32[64,2,1,128]{3,2,1,0:T(1,128)S(1)}, f32[2,192,768]{2,1,0:T(8,128)S(1)}, f32[2,192,768]{2,1,0:T(8,128)S(1)}) custom-call(s32[1,64]{1,0:T(1,128)} %bitcast.14, f32[1152,1,128]{2,1,0:T(1,128)} %bitcast.15, f32[2,192,768]{2,1,0:T(8,128)} %left_root.1, f32[2,192,768]{2,1,0:T(8,128)} %right_root.1, ...), custom_call_target="tpu_custom_call" | custom-call | tf_op jit(solution)/shard_map/pallas_call | solution.py:534
  88.8 0.0 copy-done
  88.9 0.0 copy-done.1
  88.9 2.3 %shard_map.103 = (f32[1152,128]{1,0:T(8,128)}, bf16[3,64,768]{2,1,0:T(8,128)(2,1)}, f32[2,192,768]{2,1,0:T(8,128)}, f32[2,192,768]{2,1,0:T(8,128)}) custom-call(s32[64]{0:T(128)S(1)} %copy-done.1, f32[2304,128]{1,0:T(8,128)S(1)} %bitcast.11, f32[128,128]{1,0:T(8,128)S(1)} %bitcast.13, bf16[3,64,768]{2,1,0:T(8,128)(2,1)S(1)} %bitcast.12, ...), custom_call_target="tpu_custom_call" | custom-call | tf_op jit(solution)/shard_map/pallas_call | solution.py:595
Async XLA Ops:
  0.6 88.2 %copy-start = (bf16[64,1,3,768]{3,0,2,1:T(8,128)(2,1)S(1)}, bf16[64,1,3,768]{3,0,2,1:T(8,128)(2,1)}, u32[]{:S(2)}) copy-start(bf16[64,1,3,768]{3,0,2,1:T(8,128)(2,1)} %param.8) | copy-start | bytes 884740
  0.6 88.2 %copy-start.1 = (s32[64]{0:T(128)S(1)}, s32[64]{0:T(128)}, u32[]{:S(2)}) copy-start(s32[64]{0:T(128)} %owner.1) | copy-start | bytes 772
